TPU v7x, 768 devices: a whole 4x8x12 slice. The times are simulated.
768 devices in a mesh: ctx: 16 (over x, z_hi), ch: 48 (over z_lo, y, core).
Axes of the slice: x: 4, y: 8, z: 12 (z_hi: 4, z_lo: 3; z = z_hi * 3 + z_lo), core: 2. Of those that a mesh axis runs over, the one named last changes fastest.
Arguments:
- saved_input: float32 [256, 384, 128], P('ctx', 'ch'), may hold values from -6 to 6
- out_grad: float32 [256, 384, 128], P('ctx', 'ch'), may hold values from -0.0068359375 to 0.0068359375
- filter_spec: float32 [2, 16, 256, 256], P(None, None, 'ctx'), as said below
Outputs:
- in_grad: float32 [256, 384, 128], P('ctx', 'ch')
- filter_grad: float32 [256, 16, 128], P('ctx')
Inputs may be any that keep to these rules, and one draw needn't show every extreme that they name: `filter_spec`: each filter's spectrum is that of a real sequence of 65536 terms: with k = k1 + 256 * k2, the value at frequency (-k mod 65536) is the complex conjugate of the value at k.
All inputs are finite; a program needn't handle non-finite values.
Results may differ from a plain program's by a relative error of at most 0.0003.
Values sent between devices are 32-bit elements; how exact they have to be, the bound alone decides.
A program may use at most 32 MiB of HBM per device.

v0:
```python
import math

import jax
import jax.numpy as jnp
from jax import lax
from jax.sharding import PartitionSpec as P

FULL_PRECISION = lax.Precision.HIGHEST


def phase_tables(row_ids, col_ids, period):
    product = row_ids[:, None] * col_ids[None, :] % period
    angles = product.astype(jnp.float32) * (2.0 * math.pi / period)
    return (jnp.cos(angles), jnp.sin(angles))


def gauss_product(real_part, imag_part, cos_table, sin_table, contract):
    first_term = contract(real_part + imag_part, cos_table)
    second_term = contract(real_part, sin_table - cos_table)
    third_term = contract(imag_part, cos_table + sin_table)
    return (first_term - third_term, first_term + second_term)


def body(saved_input, out_grad, filter_spec):
    ctx_count = lax.axis_size("ctx")
    ctx_place = lax.axis_index("ctx")
    ch_place = lax.axis_index("ch")
    cols_dev = saved_input.shape[0]
    channels = saved_input.shape[1]
    half_rows = saved_input.shape[2]
    radix_size = 2 * half_rows
    filter_count = filter_spec.shape[1]
    freq_dev = filter_spec.shape[2]
    padded_len = radix_size * radix_size
    full_ids = jnp.arange(radix_size, dtype=jnp.int32)
    local_ids = jnp.arange(cols_dev, dtype=jnp.int32)
    freq_ids = jnp.arange(freq_dev, dtype=jnp.int32)
    cos_full, sin_full = phase_tables(full_ids, full_ids, radix_size)
    fields = jnp.stack([saved_input, out_grad])
    cos_part = cos_full[:, :half_rows].reshape(ctx_count, freq_dev, half_rows)
    sin_part = sin_full[:, :half_rows].reshape(ctx_count, freq_dev, half_rows)
    first_real = jnp.einsum("fbca,qka->fqbck", fields, cos_part, precision=FULL_PRECISION)
    first_imag = -jnp.einsum("fbca,qka->fqbck", fields, sin_part, precision=FULL_PRECISION)
    twist_cos, twist_sin = phase_tables(ctx_place * cols_dev + local_ids, full_ids, padded_len)
    twist_cos = jnp.transpose(twist_cos.reshape(cols_dev, ctx_count, freq_dev), (1, 0, 2))[
        :, :, None, :
    ]
    twist_sin = jnp.transpose(twist_sin.reshape(cols_dev, ctx_count, freq_dev), (1, 0, 2))[
        :, :, None, :
    ]
    turned_real = first_real * twist_cos + first_imag * twist_sin
    turned_imag = first_imag * twist_cos - first_real * twist_sin
    turned = jnp.stack([turned_real, turned_imag], axis=1)
    turned = turned.reshape(2, 2, ctx_count, cols_dev, channels * freq_dev)
    neg_sin = -sin_full

    def column_contract(operand, matrix):
        return jnp.einsum("fbck,bm->fckm", operand, matrix, precision=FULL_PRECISION)

    pieces = lax.all_to_all(turned, "ctx", split_axis=2, concat_axis=3, tiled=True)
    shaped = pieces[:, :, 0].reshape(pieces.shape[0], 2, radix_size, channels, freq_dev)
    out_real, out_imag = gauss_product(
        shaped[:, 0], shaped[:, 1], cos_full, neg_sin, column_contract
    )
    spectra = jnp.stack([out_real, out_imag], axis=1)
    filter_start = ch_place * channels % filter_count
    own_filters = lax.dynamic_slice_in_dim(filter_spec, filter_start, channels, 1)
    spec_real = own_filters[0]
    spec_imag = own_filters[1]
    in_real = spectra[0, 0]
    in_imag = spectra[0, 1]
    grad_real = spectra[1, 0]
    grad_imag = spectra[1, 1]
    back_real = spec_real * grad_real + spec_imag * grad_imag
    back_imag = spec_real * grad_imag - spec_imag * grad_real
    corr_real = grad_real * in_real + grad_imag * in_imag
    corr_imag = grad_imag * in_real - grad_real * in_imag
    freq_fields = jnp.stack([jnp.stack([back_real, back_imag]), jnp.stack([corr_real, corr_imag])])
    count_fields = freq_fields.shape[0]
    inverse_cos = cos_full.reshape(radix_size, ctx_count, cols_dev)
    inverse_sin = sin_full.reshape(radix_size, ctx_count, cols_dev)

    def freq_contract(operand, matrix):
        return jnp.einsum("fckm,mqb->fqbck", operand, matrix, precision=FULL_PRECISION)

    section_real, section_imag = gauss_product(
        freq_fields[:, 0], freq_fields[:, 1], inverse_cos, inverse_sin, freq_contract
    )
    return_cos, return_sin = phase_tables(full_ids, ctx_place * freq_dev + freq_ids, padded_len)
    return_cos = return_cos.reshape(ctx_count, cols_dev, 1, freq_dev)
    return_sin = return_sin.reshape(ctx_count, cols_dev, 1, freq_dev)
    twisted_real = section_real * return_cos - section_imag * return_sin
    twisted_imag = section_imag * return_cos + section_real * return_sin
    leaving = jnp.stack([twisted_real, twisted_imag], axis=1)
    leaving = leaving.reshape(count_fields, 2, ctx_count, cols_dev, channels * freq_dev)
    row_cos = (cos_full[:half_rows] / padded_len).reshape(half_rows, ctx_count, freq_dev)
    row_sin = (sin_full[:half_rows] / padded_len).reshape(half_rows, ctx_count, freq_dev)

    def rows_contract(operand, matrix):
        return jnp.einsum("fbqck,aqk->fbca", operand, matrix, precision=FULL_PRECISION)

    pieces = lax.all_to_all(leaving, "ctx", split_axis=2, concat_axis=4, tiled=True)
    column_count = pieces.shape[3]
    shaped = pieces[:, :, 0].reshape(
        pieces.shape[0], 2, column_count, ctx_count, channels, freq_dev
    )
    real_in = shaped[:, 0]
    imag_in = shaped[:, 1]
    result = rows_contract(real_in, row_cos) - rows_contract(imag_in, row_sin)
    filter_ids = jnp.arange(filter_count, dtype=jnp.int32)
    owners = (ch_place * channels + jnp.arange(channels, dtype=jnp.int32)) % filter_count
    selector = (filter_ids[:, None] == owners[None, :]).astype(jnp.float32)
    filter_term = jnp.einsum("fc,bca->bfa", selector, result[1], precision=FULL_PRECISION)
    filter_grad = lax.psum(filter_term, "ch")
    return (result[0], filter_grad)


def solution(mesh):
    placed = (P("ctx", "ch", None), P("ctx", "ch", None), P(None, None, "ctx", None))
    return jax.shard_map(
        body,
        mesh=mesh,
        in_specs=placed,
        out_specs=(P("ctx", "ch", None), P("ctx", None, None)),
        check_vma=False,
    )
```

profile of v0, /device:TPU:198, one launch (start us, length us, event | category | flops | bytes accessed | tf_op | source)
XLA Modules:
  0.0 519.8 jit_solution(12523728115852819933)
XLA Ops:
  7.2 1.0 fusion.56
  8.1 1.0 fusion.55
  9.4 0.9 copy_bitcast_fusion
  10.3 1.1 fusion.72
  11.4 1.8 fusion.69
  13.2 3.5 fusion.4
  16.7 2.2 copy.34
  19.5 0.8 pad_maximum_fusion
  20.3 14.7 %all-to-all-start = ((f32[2,2,16,16,128]{4,3,1,0,2:T(8,128)}), f32[2,2,16,16,128]{4,3,1,0,2:T(8,128)S(1)}, u32[]{:S(2)}, u32[]{:S(2)}) async-start(f32[2,2,16,16,128]{4,3,1,0,2:T(8,128)} %pad_maximum_fusion), calls=%async_computation | async-start | bytes 1048576 | tf_op jit(solution)/shard_map/all_to_all | solution.py:60
  35.2 17.9 %all-to-all-done = f32[2,2,16,16,128]{4,3,1,0,2:T(8,128)S(1)} async-done(((f32[2,2,16,16,128]{4,3,1,0,2:T(8,128)}), f32[2,2,16,16,128]{4,3,1,0,2:T(8,128)S(1)}, u32[]{:S(2)}, u32[]{:S(2)}) %all-to-all-start) | async-done | bytes 524320 | tf_op jit(solution)/shard_map/all_to_all | solution.py:60
  53.2 2.8 copy.71
  56.0 3.5 reshape.248
  59.5 1.4 fusion.31
  60.9 1.4 convolution_add_fusion.1
  62.3 1.4 convolution_subtract_fusion.1
  63.9 2.8 fusion.24
  66.7 2.9 convolution_add_fusion
  69.6 5.0 subtract_bitcast_fusion
  74.6 0.9 copy.44
  76.1 2.5 copy.45
  79.1 0.8 copy.46
  80.0 9.6 %all-to-all-start.1 = ((f32[2,2,16,16,128]{4,3,0,1,2:T(8,128)}), f32[2,2,16,16,128]{4,3,0,1,2:T(8,128)S(1)}, u32[]{:S(2)}, u32[]{:S(2)}) async-start(f32[2,2,16,16,128]{4,3,0,1,2:T(8,128)} %copy.46), calls=%async_computation.1 | async-start | bytes 1048576 | tf_op jit(solution)/shard_map/all_to_all | solution.py:102
  89.6 12.9 %all-to-all-done.1 = f32[2,2,16,16,128]{4,3,0,1,2:T(8,128)S(1)} async-done(((f32[2,2,16,16,128]{4,3,0,1,2:T(8,128)}), f32[2,2,16,16,128]{4,3,0,1,2:T(8,128)S(1)}, u32[]{:S(2)}, u32[]{:S(2)}) %all-to-all-start.1) | async-done | bytes 524320 | tf_op jit(solution)/shard_map/all_to_all | solution.py:102
  102.5 2.6 reshape.249
  105.1 4.7 fusion.110
  109.8 2.5 copy.76
  112.3 3.4 copy.75
  115.7 3.4 fusion.6
  119.1 1.8 fusion.12
  121.0 1.0 convolution_bitcast_fusion
  122.6 388.8 %all-reduce.2.cloned.1.call-done = f32[16,16,128]{2,1,0:T(8,128)} async-done(((f32[16,16,128]{2,1,0:T(8,128)}), f32[16,16,128]{2,1,0:T(8,128)}) %all-reduce.2.cloned.1.call-update) | async-done | bytes 131088 | tf_op jit(solution)/shard_map/psum | solution.py:114
  511.4 1.6 copy.84
  (23 shorter events, 3.0 us)
Async XLA Ops:
  20.3 32.9 %all-to-all-start = ((f32[2,2,16,16,128]{4,3,1,0,2:T(8,128)}), f32[2,2,16,16,128]{4,3,1,0,2:T(8,128)S(1)}, u32[]{:S(2)}, u32[]{:S(2)}) async-start(f32[2,2,16,16,128]{4,3,1,0,2:T(8,128)} %pad_maximum_fusion), calls=%async_computation | async-start | bytes 1048576 | tf_op jit(solution)/shard_map/all_to_all | solution.py:60
  59.5 4.3 copy-start
  80.0 22.5 %all-to-all-start.1 = ((f32[2,2,16,16,128]{4,3,0,1,2:T(8,128)}), f32[2,2,16,16,128]{4,3,0,1,2:T(8,128)S(1)}, u32[]{:S(2)}, u32[]{:S(2)}) async-start(f32[2,2,16,16,128]{4,3,0,1,2:T(8,128)} %copy.46), calls=%async_computation.1 | async-start | bytes 1048576 | tf_op jit(solution)/shard_map/all_to_all | solution.py:102
  89.5 421.9 %all-reduce.2.cloned.1.call-start = ((), (), s32[]{:S(2)}) async-start(), calls=%async_computation.2 | async-start | bytes 262144 | tf_op jit(solution)/shard_map/psum | solution.py:114
Sparse Core Ops, SparseCore 0:
  122.1 389.2 all-reduce.1
where the time goes:
time: 520 us
  waiting for transfers between devices  420 us (81%)
  local copies, waits for them, and re-layouts  31 us (6%)
  matrix products  26.5 us (5%)
  starting transfers between devices  24.3 us (5%)
  between operations  14.3 us (3%)
    psum x1, waiting for transfers between devices, body(): filter_grad = lax.psum(filter_term, 'ch')  389 us
    all_to_all x1, waiting for transfers between devices, body(): lax.all_to_all(turned, 'ctx', split_axis=2, concat_axis=3, tiled=True)  17.9 us
    all_to_all x1, starting transfers between devices, body(): lax.all_to_all(turned, 'ctx', split_axis=2, concat_axis=3, tiled=True)  14.7 us
    all_to_all x1, waiting for transfers between devices, body(): lax.all_to_all(leaving, 'ctx', split_axis=2, concat_axis=4, tiled=True)  12.9 us
    dot_general x3, matrix products, freq_contract(): jnp.einsum('fckm,mqb->fqbck', operand, matrix, precision=FULL_PRECISION)  10.7 us
  transfers between devices with their start and end apart: 3, of which 3 were waited for; matrix products, arithmetic and copies ran while one was open for 0% of the time, Pallas kernels for 0%

commit v1 on v0

v1 whole, which is shorter than its diff:
```python
import functools
import math

import jax
import jax.numpy as jnp
import ml_dtypes
import numpy as np
from jax import lax
from jax.experimental import pallas as pl
from jax.experimental.pallas import tpu as pltpu
from jax.sharding import PartitionSpec as P

MESH = pl.DeviceIdType.MESH
RADIX = 256
HALF = 128
PADDED = RADIX * RADIX
NCTX = 16
COLS = 16
CHAN = 8
SLOTS = 8
YS = 8
GROUP = 16
ZS = 3
SPECIAL = 8
F32 = jnp.float32
BF16 = jnp.bfloat16


def split_np(table):
    high = table.astype(np.float32).astype(ml_dtypes.bfloat16)
    low = (table - high.astype(np.float64)).astype(np.float32).astype(ml_dtypes.bfloat16)
    return np.stack([high, low])


def slot_freqs():
    q = np.arange(NCTX)[:, None]
    s = np.arange(SLOTS)[None, :]
    return np.where(q < 8, 16 * q + s, 16 * q + 1 + s)


def angle(product, period):
    return (product % period).astype(np.float64) * (2.0 * math.pi / period)


def tables():
    k1 = slot_freqs()
    a = np.arange(HALF)
    b = np.arange(RADIX)
    alt = 1.0 - 2.0 * (a % 2)
    ang = angle(k1[:, :, None] * a[None, None, :], RADIX)
    first = np.stack([np.cos(ang), -np.sin(ang)], axis=1)
    first[0, 1, 0] = alt
    first = split_np(first.reshape(RADIX, HALF))
    weight = np.full((NCTX, SLOTS, 1), 2.0)
    weight[0, 0] = 1.0
    last = np.stack([weight * np.cos(ang), -weight * np.sin(ang)], axis=1)
    last[0, 1, 0] = alt
    last = split_np(np.ascontiguousarray(last.reshape(RADIX, HALF).T) / PADDED)
    both = angle(b[:, None] * b[None, :], RADIX)
    square = split_np(np.concatenate([np.cos(both), np.sin(both)], axis=1))
    bp = b.reshape(NCTX, COLS)
    lanes = np.tile(bp, (1, CHAN))
    rows = np.concatenate([k1.reshape(-1), np.full(8, HALF)])
    turn = angle(rows[None, :, None] * lanes[:, None, :], PADDED)
    turn = np.stack([np.cos(turn), np.sin(turn)], axis=1).astype(np.float32)
    rows2 = np.concatenate([k1, np.full((NCTX, 8), HALF)], axis=1)
    back = angle(rows2[:, :, None] * b[None, None, :], PADDED)
    back = np.stack([np.cos(back), np.sin(back)], axis=1).astype(np.float32)
    return first, turn, square, back, last


def split(values):
    high = values.astype(BF16)
    low = (values - high.astype(F32)).astype(BF16)
    return high, low


def dot(x, y, dims=((1,), (0,))):
    return lax.dot_general(x, y, (dims, ((), ())), preferred_element_type=F32)


def dot3(x, y, dims=((1,), (0,))):
    return dot(x[0], y[0], dims) + (dot(x[1], y[0], dims) + dot(x[0], y[1], dims))


def block_transpose(parts, lane):
    parts = list(parts)
    for d in (1, 2, 4):
        odd = (lane & (16 * d)) != 0
        fresh = list(parts)
        for j in range(8):
            if j & d == 0:
                lo, hi = parts[j], parts[j + d]
                fresh[j] = jnp.where(odd, pltpu.roll(hi, 16 * d, 1), lo)
                fresh[j + d] = jnp.where(odd, hi, pltpu.roll(lo, 128 - 16 * d, 1))
        parts = fresh
    return parts


def kernel(
    full,
    u_ref, g_ref, h_hbm, first_ref, turn_hbm, square_ref, back_hbm, last_ref,
    in_out, filt_out,
    h_ref, turn_ref, back_ref, send1, recv1, send2, recv2, ext, ext2,
    part, gathered, zpart, everyone,
    local_sem, s1, r1, e1s, e1r, s2, r2, e2s, e2r, rs_s, rs_r, z_s, z_r, ag_s, ag_r,
):
    q = lax.axis_index("ctx")
    ch = lax.axis_index("ch")
    m = ch % GROUP
    zl = ch // GROUP
    core = m % 2
    y = m // 2

    copies = [
        pltpu.make_async_copy(turn_hbm.at[q], turn_ref, local_sem.at[0]),
        pltpu.make_async_copy(h_hbm.at[:, pl.ds(core * CHAN, CHAN)], h_ref, local_sem.at[1]),
        pltpu.make_async_copy(back_hbm.at[q], back_ref, local_sem.at[2]),
    ]
    for copy in copies:
        copy.start()
    recv1[...] = jnp.zeros_like(recv1)
    send1[:, 4] = jnp.zeros((NCTX, 8, HALF), F32)
    ext[...] = jnp.zeros_like(ext)

    barrier = pltpu.get_barrier_semaphore()

    def at_ctx(p):
        return (p, ch)

    def at_group(mm):
        return (q, zl * GROUP + mm)

    def at_z(zz):
        return (q, zz * GROUP + m)

    def greet(device):
        pl.semaphore_signal(barrier, inc=1, device_id=device, device_id_type=MESH)

    def each(count, fn):
        def step(d, carry):
            fn(d)
            return carry

        lax.fori_loop(1, count, step, 0)

    each(NCTX, lambda d: greet(at_ctx((q + d) % NCTX)))
    if full:
        each(GROUP, lambda d: greet(at_group((m + d) % GROUP)))
        each(ZS, lambda d: greet(at_z((zl + d) % ZS)))

    def remote(src, dst, ss, rs, device):
        return pltpu.make_async_remote_copy(
            src_ref=src, dst_ref=dst, send_sem=ss, recv_sem=rs,
            device_id=device, device_id_type=MESH,
        )

    rows = [ref[:, c, :] for ref in (u_ref, g_ref) for c in range(CHAN)]
    x = split(jnp.concatenate(rows, axis=0))
    y1 = dot3((first_ref[0], first_ref[1]), x, ((1,), (1,))).reshape(NCTX, 2, SLOTS, RADIX)
    copies[0].wait()
    sub = lax.broadcasted_iota(jnp.int32, (SLOTS, HALF), 0)
    keep = (lax.broadcasted_iota(jnp.int32, (NCTX, SLOTS, HALF), 0)
            + lax.broadcasted_iota(jnp.int32, (NCTX, SLOTS, HALF), 1)) > 0
    tc = turn_ref[0, :HALF].reshape(NCTX, SLOTS, HALF)
    ts = turn_ref[1, :HALF].reshape(NCTX, SLOTS, HALF)
    ec, es = turn_ref[0, HALF:], turn_ref[1, HALF:]
    extra = jnp.zeros((SLOTS, HALF), F32)
    for f in range(2):
        lanes = slice(f * HALF, (f + 1) * HALF)
        re = y1[:, 0, :, lanes]
        im = y1[:, 1, :, lanes]
        mid = jnp.broadcast_to(im[0, 0:1, :], (SLOTS, HALF))
        extra = jnp.where(sub == 2 * f, mid * ec, extra)
        extra = jnp.where(sub == 2 * f + 1, -mid * es, extra)
        im = jnp.where(keep, im, 0.0)
        send1[:, 2 * f] = re * tc + im * ts
        send1[:, 2 * f + 1] = im * tc - re * ts
    send1[SPECIAL, 4] = extra
    recv1[q] = send1[q]

    peers = NCTX - 1 + ((GROUP - 1 + ZS - 1) if full else 0)
    pl.semaphore_wait(barrier, peers)

    def main1(p):
        return remote(send1.at[p, pl.ds(0, 4)], recv1.at[q, pl.ds(0, 4)], s1.at[p], r1.at[q], at_ctx(p))

    def from1(p):
        return remote(send1.at[p, pl.ds(0, 4)], recv1.at[p, pl.ds(0, 4)], s1.at[p], r1.at[p], at_ctx(p))

    each(NCTX, lambda d: main1((q + d) % NCTX).start())

    ext_send1 = remote(send1.at[SPECIAL, 4], recv1.at[q, 4], e1s.at[0], e1r.at[q], at_ctx(SPECIAL))

    @pl.when(q != SPECIAL)
    def _():
        ext_send1.start()

    copies[1].wait()
    copies[2].wait()
    each(NCTX, lambda d: from1((q + d) % NCTX).wait_recv())

    @pl.when(q == SPECIAL)
    def _():
        each(NCTX, lambda d: remote(
            send1.at[SPECIAL, 4], recv1.at[(q + d) % NCTX, 4], e1s.at[0],
            e1r.at[(q + d) % NCTX], at_ctx((q + d) % NCTX)).wait_recv())

    lane = lax.broadcasted_iota(jnp.int32, (40, HALF), 1)
    halves = [
        block_transpose([recv1[8 * h + j].reshape(40, HALF) for j in range(8)], lane)
        for h in range(2)
    ]
    per_c = [jnp.concatenate([halves[0][c], halves[1][c]], axis=1) for c in range(CHAN)]
    for c in range(CHAN):
        ext[c] = per_c[c][32:40]
    planes = [per_c[c][8 * r : 8 * r + 8] for r in range(4) for c in range(CHAN)]
    planes += [ext[:, r, :] for r in range(4)]
    square = (square_ref[0], square_ref[1])
    spec = dot3(split(jnp.concatenate(planes, axis=0)), square)

    def take(values, r):
        return values[64 * r : 64 * r + 64], values[256 + 8 * r : 256 + 8 * r + 8]

    def forward(values, r):
        out = []
        for re, im in zip(take(values, r), take(values, r + 1)):
            out.append((re[:, :RADIX] + im[:, RADIX:], im[:, :RADIX] - re[:, RADIX:]))
        return out

    us, gs = forward(spec, 0), forward(spec, 2)
    low = q < NCTX // 2
    hr = jnp.where(low, h_ref[0, :, 0:8, :], h_ref[0, :, 1:9, :]).reshape(64, RADIX)
    hi = jnp.where(low, h_ref[1, :, 0:8, :], h_ref[1, :, 1:9, :]).reshape(64, RADIX)
    hs = [(hr, hi), (h_ref[0, :, 0, :], h_ref[1, :, 0, :])]
    groups = []
    for (ar, ai), (gr, gi), (fr, fi) in zip(us, gs, hs):
        groups.append((fr * gr + fi * gi, fr * gi - fi * gr, gr * ar + gi * ai, gi * ar - gr * ai))
    inv = dot3(split(jnp.concatenate(groups[0] + groups[1], axis=0)), square)
    bc, bs = back_ref[0, :8], back_ref[1, :8]
    xc, xs = back_ref[0, 8:], back_ref[1, 8:]
    outs = []
    for f in range(2):
        (re, xr), (im, xi) = take(inv, 2 * f), take(inv, 2 * f + 1)
        qr = (re[:, :RADIX] - im[:, RADIX:]).reshape(CHAN, SLOTS, RADIX)
        qi = (im[:, :RADIX] + re[:, RADIX:]).reshape(CHAN, SLOTS, RADIX)
        outs.append(qr * bc[None] - qi * bs[None])
        outs.append(qi * bc[None] + qr * bs[None])
        er = xr[:, :RADIX] - xi[:, RADIX:]
        ei = xi[:, :RADIX] + xr[:, RADIX:]
        ext2[:, f, :] = er * xc - ei * xs
    for r in range(2, 8):
        ext2[:, r, :] = jnp.zeros((CHAN, RADIX), F32)
    per_c = [jnp.concatenate([o[c] for o in outs] + [ext2[c]], axis=0) for c in range(CHAN)]
    for h in range(2):
        for j, value in enumerate(block_transpose([v[:, h * HALF : (h + 1) * HALF] for v in per_c], lane)):
            send2[8 * h + j] = value.reshape(5, 8, HALF)
    recv2[q, 0:4] = send2[q, 0:4]

    def main2(p):
        return remote(send2.at[p, pl.ds(0, 4)], recv2.at[q, pl.ds(0, 4)], s2.at[p], r2.at[q], at_ctx(p))

    def from2(p):
        return remote(send2.at[p, pl.ds(0, 4)], recv2.at[p, pl.ds(0, 4)], s2.at[p], r2.at[p], at_ctx(p))

    def extra2(p):
        return remote(send2.at[p, 4], recv2.at[SPECIAL, 4], e2s.at[p], e2r.at[0], at_ctx(p))

    @pl.when(q == SPECIAL)
    def _():
        recv2[SPECIAL, 4] = send2[SPECIAL, 4]
        each(NCTX, lambda d: extra2((q + d) % NCTX).start())

    each(NCTX, lambda d: main2((q + d) % NCTX).start())
    each(NCTX, lambda d: from2((q + d) % NCTX).wait_recv())

    @pl.when(q != SPECIAL)
    def _():
        remote(send2.at[0, 4], recv2.at[SPECIAL, 4], e2s.at[0], e2r.at[0], at_ctx(SPECIAL)).wait_recv()

    for f in range(2):
        recv2[0, 2 * f + 1, 0:1, :] = recv2[SPECIAL, 4, f : f + 1, :]
    both = jnp.concatenate(
        [recv2[:, 2 * f : 2 * f + 2].reshape(RADIX, HALF) for f in range(2)], axis=1
    )
    result = dot3((last_ref[0], last_ref[1]), split(both))
    own = result[:, :HALF].T
    for c in range(CHAN):
        in_out[:, c, :] = own[COLS * c : COLS * (c + 1)]
    part[...] = result[:, HALF:].T.reshape(CHAN, COLS, HALF)

    if full:
        def out_rs(yy):
            return remote(part.at[yy], gathered.at[y], rs_s.at[yy], rs_r.at[y], at_group(yy * 2 + core))

        def in_rs(yy):
            return remote(part.at[yy], gathered.at[yy], rs_s.at[yy], rs_r.at[yy], at_group(yy * 2 + core))

        each(YS, lambda d: out_rs((y + d) % YS).start())
        gathered[y] = part[y]
        each(YS, lambda d: in_rs((y + d) % YS).wait_recv())
        zpart[zl] = jnp.sum(gathered[...], axis=0)

        def out_z(zz):
            return remote(zpart.at[zl], zpart.at[zl], z_s.at[zz], z_r.at[zl], at_z(zz))

        def in_z(zz):
            return remote(zpart.at[zz], zpart.at[zz], z_s.at[zz], z_r.at[zz], at_z(zz))

        each(ZS, lambda d: out_z((zl + d) % ZS).start())
        each(ZS, lambda d: in_z((zl + d) % ZS).wait_recv())
        fid = core * CHAN + y
        everyone[fid] = (zpart[0] + zpart[1]) + zpart[2]

        def out_ag(mm):
            return remote(everyone.at[fid], everyone.at[fid], ag_s.at[mm], ag_r.at[m], at_group(mm))

        def in_ag(mm):
            other = (mm % 2) * CHAN + mm // 2
            return remote(everyone.at[other], everyone.at[other], ag_s.at[mm], ag_r.at[mm], at_group(mm))

        each(GROUP, lambda d: out_ag((m + d) % GROUP).start())
        each(GROUP, lambda d: in_ag((m + d) % GROUP).wait_recv())
        for f in range(2 * CHAN):
            filt_out[:, f, :] = everyone[f]
        each(YS, lambda d: out_rs((y + d) % YS).wait_send())
        each(ZS, lambda d: out_z((zl + d) % ZS).wait_send())
        each(GROUP, lambda d: out_ag((m + d) % GROUP).wait_send())
    else:
        for f in range(2 * CHAN):
            filt_out[:, f, :] = part[f % CHAN]

    each(NCTX, lambda d: main1((q + d) % NCTX).wait_send())
    each(NCTX, lambda d: main2((q + d) % NCTX).wait_send())

    @pl.when(q != SPECIAL)
    def _():
        ext_send1.wait_send()

    @pl.when(q == SPECIAL)
    def _():
        each(NCTX, lambda d: extra2((q + d) % NCTX).wait_send())


def body(saved_input, out_grad, filter_spec):
    full = lax.axis_size("ch") > 1
    first, turn, square, back, last = (jnp.asarray(t) for t in tables())
    vm = pl.BlockSpec(memory_space=pltpu.VMEM)
    hbm = pl.BlockSpec(memory_space=pl.ANY)
    sem = pltpu.SemaphoreType.DMA
    v = pltpu.VMEM
    return pl.pallas_call(
        functools.partial(kernel, full),
        out_shape=(
            jax.ShapeDtypeStruct((COLS, CHAN, HALF), F32),
            jax.ShapeDtypeStruct((COLS, 2 * CHAN, HALF), F32),
        ),
        in_specs=[vm, vm, hbm, vm, hbm, vm, hbm, vm],
        out_specs=(vm, vm),
        scratch_shapes=[
            v((2, CHAN, 16, RADIX), F32),
            v((2, HALF + 8, HALF), F32),
            v((2, 16, RADIX), F32),
            v((NCTX, 5, SLOTS, HALF), F32),
            v((NCTX, 5, SLOTS, HALF), F32),
            v((NCTX, 5, SLOTS, HALF), F32),
            v((NCTX, 5, SLOTS, HALF), F32),
            v((CHAN, 8, RADIX), F32),
            v((CHAN, 8, RADIX), F32),
            v((CHAN, COLS, HALF), F32),
            v((YS, COLS, HALF), F32),
            v((ZS, COLS, HALF), F32),
            v((2 * CHAN, COLS, HALF), F32),
            sem((3,)),
            sem((NCTX,)), sem((NCTX,)), sem((1,)), sem((NCTX,)),
            sem((NCTX,)), sem((NCTX,)), sem((NCTX,)), sem((1,)),
            sem((YS,)), sem((YS,)), sem((ZS,)), sem((ZS,)), sem((GROUP,)), sem((GROUP,)),
        ],
        compiler_params=pltpu.CompilerParams(
            collective_id=0, has_side_effects=True, vmem_limit_bytes=24 * 2**20
        ),
        cost_estimate=pl.CostEstimate(flops=400_000_000, bytes_accessed=2_000_000, transcendentals=0),
    )(saved_input, out_grad, filter_spec, first, turn, square, back, last)


def solution(mesh):
    placed = (P("ctx", "ch", None), P("ctx", "ch", None), P(None, None, "ctx", None))
    return jax.shard_map(
        body,
        mesh=mesh,
        in_specs=placed,
        out_specs=(P("ctx", "ch", None), P("ctx", None, None)),
        check_vma=False,
    )
```

time: 520 us -> 71.3 us (0.14)
  the two profiles are of different devices: /device:TPU:198 before, /device:TPU:1 now
where the time goes in v1:
time: 71.3 us; the launch traced here: 70.9 us
  Pallas kernels  60.7 us (85%)
  local copies, waits for them, and re-layouts  9.52 us (13%)
    pallas_call x1, Pallas kernels, body(): pl.pallas_call(functools.partial(kernel, full), out_shape=(jax.ShapeDtype...  60.7 us
    unnamed x18, local copies, waits for them, and re-layouts  9.52 us

profile of v1, /device:TPU:1, one launch (start us, length us, event | category | flops | bytes accessed | tf_op | source)
XLA Modules:
  0.0 70.9 jit_solution(11973261243028393274)
XLA Ops:
  0.6 0.0 copy-start
  0.6 1.6 %copy-done = f32[16,2,136,128]{3,2,1,0:T(8,128)S(1)} copy-done((f32[16,2,136,128]{3,2,1,0:T(8,128)S(1)}, f32[16,2,136,128]{3,2,1,0:T(8,128)}, u32[]{:S(2)}) %copy-start) | copy-done | bytes 2228248
  2.3 0.0 copy-start.1
  2.3 1.0 %copy-done.1 = f32[2,16,16,256]{3,2,1,0:T(8,128)S(1)} copy-done((f32[2,16,16,256]{3,2,1,0:T(8,128)S(1)}, f32[2,16,16,256]{3,2,1,0:T(8,128)}, u32[]{:S(2)}) %copy-start.1) | copy-done | bytes 524312
  3.3 0.0 copy-start.2
  3.3 1.0 %copy-done.2 = f32[16,2,16,256]{3,2,1,0:T(8,128)S(1)} copy-done((f32[16,2,16,256]{3,2,1,0:T(8,128)S(1)}, f32[16,2,16,256]{3,2,1,0:T(8,128)}, u32[]{:S(2)}) %copy-start.2) | copy-done | bytes 524312
  4.3 0.0 copy-start.3
  4.3 1.0 %copy-done.3 = bf16[2,256,512]{2,1,0:T(8,128)(2,1)S(1)} copy-done((bf16[2,256,512]{2,1,0:T(8,128)(2,1)S(1)}, bf16[2,256,512]{2,1,0:T(8,128)(2,1)}, u32[]{:S(2)}) %copy-start.3) | copy-done | bytes 524312
  5.4 0.0 copy-start.4
  5.4 0.9 %copy-done.4 = bf16[2,128,256]{2,1,0:T(8,128)(2,1)S(1)} copy-done((bf16[2,128,256]{2,1,0:T(8,128)(2,1)S(1)}, bf16[2,128,256]{2,1,0:T(8,128)(2,1)}, u32[]{:S(2)}) %copy-start.4) | copy-done | bytes 131096
  6.3 0.0 copy-start.5
  6.3 0.9 %copy-done.5 = bf16[2,256,128]{2,1,0:T(8,128)(2,1)S(1)} copy-done((bf16[2,256,128]{2,1,0:T(8,128)(2,1)S(1)}, bf16[2,256,128]{2,1,0:T(8,128)(2,1)}, u32[]{:S(2)}) %copy-start.5) | copy-done | bytes 131096
  7.2 0.0 copy-start.6
  7.2 0.8 %copy-done.6 = f32[16,8,128]{2,1,0:T(8,128)S(1)} copy-done((f32[16,8,128]{2,1,0:T(8,128)S(1)}, f32[16,8,128]{2,1,0:T(8,128)}, u32[]{:S(2)}) %copy-start.6) | copy-done | bytes 65560
  8.0 0.0 copy-start.7
  8.0 0.8 %copy-done.7 = f32[16,8,128]{2,1,0:T(8,128)S(1)} copy-done((f32[16,8,128]{2,1,0:T(8,128)S(1)}, f32[16,8,128]{2,1,0:T(8,128)}, u32[]{:S(2)}) %copy-start.7) | copy-done | bytes 65560
  8.9 60.7 %shard_map.95 = (f32[16,8,128]{2,1,0:T(8,128)S(1)}, f32[16,16,128]{2,1,0:T(8,128)S(1)}) custom-call(f32[16,8,128]{2,1,0:T(8,128)S(1)} %copy-done.6, f32[16,8,128]{2,1,0:T(8,128)S(1)} %copy-done.7, f32[2,16,16,256]{3,2,1,0:T(8,128)S(1)} %copy-done.1, bf16[2,256,128]{2,1,0:T(8,128)(2,1)S(1)} %copy-done.5, f32[16,2,136,128]{3,2,1,0:T(8,128)S(1)} %copy-done, ...), custom_call_target="tpu_custom_call" | custom-call | flops 400000000 | bytes 2000000 | tf_op jit(solution)/shard_map/pallas_call | solution.py:352
  69.6 0.6 copy.12
  70.2 0.7 copy.13
Async XLA Ops:
  0.6 1.6 %copy-start = (f32[16,2,136,128]{3,2,1,0:T(8,128)S(1)}, f32[16,2,136,128]{3,2,1,0:T(8,128)}, u32[]{:S(2)}) copy-start(f32[16,2,136,128]{3,2,1,0:T(8,128)} %constant.11.clone.turn_hbm) | copy-start | bytes 6684676
  2.3 1.0 %copy-start.1 = (f32[2,16,16,256]{3,2,1,0:T(8,128)S(1)}, f32[2,16,16,256]{3,2,1,0:T(8,128)}, u32[]{:S(2)}) copy-start(f32[2,16,16,256]{3,2,1,0:T(8,128)} %h_hbm.1) | copy-start | bytes 1572868
  3.3 1.0 %copy-start.2 = (f32[16,2,16,256]{3,2,1,0:T(8,128)S(1)}, f32[16,2,16,256]{3,2,1,0:T(8,128)}, u32[]{:S(2)}) copy-start(f32[16,2,16,256]{3,2,1,0:T(8,128)} %constant.13.clone.back_hbm) | copy-start | bytes 1572868
  4.3 1.0 %copy-start.3 = (bf16[2,256,512]{2,1,0:T(8,128)(2,1)S(1)}, bf16[2,256,512]{2,1,0:T(8,128)(2,1)}, u32[]{:S(2)}) copy-start(bf16[2,256,512]{2,1,0:T(8,128)(2,1)} %constant.12.clone.square_ref) | copy-start | bytes 1572868
  5.4 0.9 %copy-start.4 = (bf16[2,128,256]{2,1,0:T(8,128)(2,1)S(1)}, bf16[2,128,256]{2,1,0:T(8,128)(2,1)}, u32[]{:S(2)}) copy-start(bf16[2,128,256]{2,1,0:T(8,128)(2,1)} %constant.14.clone.last_ref) | copy-start | bytes 393220
  6.3 0.9 %copy-start.5 = (bf16[2,256,128]{2,1,0:T(8,128)(2,1)S(1)}, bf16[2,256,128]{2,1,0:T(8,128)(2,1)}, u32[]{:S(2)}) copy-start(bf16[2,256,128]{2,1,0:T(8,128)(2,1)} %constant.10.clone.first_ref) | copy-start | bytes 393220
  7.2 0.8 %copy-start.6 = (f32[16,8,128]{2,1,0:T(8,128)S(1)}, f32[16,8,128]{2,1,0:T(8,128)}, u32[]{:S(2)}) copy-start(f32[16,8,128]{2,1,0:T(8,128)} %u_ref.1) | copy-start | bytes 196612
  8.0 0.8 %copy-start.7 = (f32[16,8,128]{2,1,0:T(8,128)S(1)}, f32[16,8,128]{2,1,0:T(8,128)}, u32[]{:S(2)}) copy-start(f32[16,8,128]{2,1,0:T(8,128)} %g_ref.1) | copy-start | bytes 196612

commit v2 on v1

v2 whole, which is shorter than its diff:
```python
import functools
import math

import jax
import jax.numpy as jnp
import ml_dtypes
import numpy as np
from jax import lax
from jax.experimental import pallas as pl
from jax.experimental.pallas import tpu as pltpu
from jax.sharding import PartitionSpec as P

MESH = pl.DeviceIdType.MESH
RADIX = 256
HALF = 128
PADDED = RADIX * RADIX
NCTX = 16
COLS = 16
CHAN = 8
SLOTS = 8
YS = 8
GROUP = 16
ZS = 3
SPECIAL = 8
F32 = jnp.float32
BF16 = jnp.bfloat16


def split_np(table):
    high = table.astype(np.float32).astype(ml_dtypes.bfloat16)
    low = (table - high.astype(np.float64)).astype(np.float32).astype(ml_dtypes.bfloat16)
    return np.stack([high, low])


def slot_freqs():
    q = np.arange(NCTX)[:, None]
    s = np.arange(SLOTS)[None, :]
    return np.where(q < 8, 16 * q + s, 16 * q + 1 + s)


def angle(product, period):
    return (product % period).astype(np.float64) * (2.0 * math.pi / period)


def tables():
    k1 = slot_freqs()
    a = np.arange(HALF)
    b = np.arange(RADIX)
    alt = 1.0 - 2.0 * (a % 2)
    ang = angle(k1[:, :, None] * a[None, None, :], RADIX)
    first = np.stack([np.cos(ang), -np.sin(ang)], axis=1)
    first[0, 1, 0] = alt
    first = split_np(first.reshape(RADIX, HALF))
    weight = np.full((NCTX, SLOTS, 1), 2.0)
    weight[0, 0] = 1.0
    last = np.stack([weight * np.cos(ang), -weight * np.sin(ang)], axis=1)
    last[0, 1, 0] = alt
    last = split_np(np.ascontiguousarray(last.reshape(RADIX, HALF).T) / PADDED)
    both = angle(b[:, None] * b[None, :], RADIX)
    square = split_np(np.concatenate([np.cos(both), np.sin(both)], axis=1))
    bp = b.reshape(NCTX, COLS)
    lanes = np.tile(bp, (1, CHAN))
    rows = np.concatenate([k1.reshape(-1), np.full(8, HALF)])
    turn = angle(rows[None, :, None] * lanes[:, None, :], PADDED)
    turn = np.stack([np.cos(turn), np.sin(turn)], axis=1).astype(np.float32)
    rows2 = np.concatenate([k1, np.full((NCTX, 8), HALF)], axis=1)
    back = angle(rows2[:, :, None] * b[None, None, :], PADDED)
    back = np.stack([np.cos(back), np.sin(back)], axis=1).astype(np.float32)
    return first, turn, square, back, last


def split(values):
    high = values.astype(BF16)
    low = (values - high.astype(F32)).astype(BF16)
    return high, low


def dot(x, y, dims=((1,), (0,))):
    return lax.dot_general(x, y, (dims, ((), ())), preferred_element_type=F32)


def dot3(x, y, dims=((1,), (0,))):
    return dot(x[0], y[0], dims) + (dot(x[1], y[0], dims) + dot(x[0], y[1], dims))


def block_transpose(parts, lane):
    parts = list(parts)
    for d in (1, 2, 4):
        odd = (lane & (16 * d)) != 0
        fresh = list(parts)
        for j in range(8):
            if j & d == 0:
                lo, hi = parts[j], parts[j + d]
                fresh[j] = jnp.where(odd, pltpu.roll(hi, 16 * d, 1), lo)
                fresh[j + d] = jnp.where(odd, hi, pltpu.roll(lo, 128 - 16 * d, 1))
        parts = fresh
    return parts


def kernel(
    full,
    u_ref, g_ref, h_hbm, first_hbm, turn_hbm, square_hbm, back_hbm, last_hbm,
    in_out, filt_out,
    first_ref, square_ref, last_ref,
    h_ref, turn_ref, back_ref, send1, recv1, send2, recv2, ext, ext2,
    part, gathered, zpart, everyone,
    local_sem, s1, r1, s2, r2, rs_s, rs_r, z_s, z_r, ag_s, ag_r, c_s, c_r,
):
    q = lax.axis_index("ctx")
    ch = lax.axis_index("ch")
    m = ch % GROUP
    zl = ch // GROUP
    core = m % 2
    y = m // 2

    copies = [
        pltpu.make_async_copy(first_hbm, first_ref, local_sem.at[0]),
        pltpu.make_async_copy(turn_hbm.at[q], turn_ref, local_sem.at[1]),
        pltpu.make_async_copy(square_hbm, square_ref, local_sem.at[2]),
        pltpu.make_async_copy(h_hbm.at[:, pl.ds(core * CHAN, CHAN)], h_ref, local_sem.at[3]),
        pltpu.make_async_copy(back_hbm.at[q], back_ref, local_sem.at[4]),
        pltpu.make_async_copy(last_hbm, last_ref, local_sem.at[5]),
    ]
    for copy in copies[:2]:
        copy.start()
    recv1[:, 4] = jnp.zeros((NCTX, SLOTS, HALF), F32)

    barrier = pltpu.get_barrier_semaphore()

    def at_ctx(p):
        return (p, ch)

    def at_group(mm):
        return (q, zl * GROUP + mm)

    def at_z(zz):
        return (q, zz * GROUP + m)

    def greet(device):
        pl.semaphore_signal(barrier, inc=1, device_id=device, device_id_type=MESH)

    def each(count, fn):
        def step(d, carry):
            fn(d)
            return carry

        lax.fori_loop(1, count, step, 0)

    each(NCTX, lambda d: greet(at_ctx((q + d) % NCTX)))
    if full:
        each(YS, lambda d: greet(at_group((y + d) % YS * 2 + core)))
        greet(at_group(m + 1 - 2 * core))
        each(ZS, lambda d: greet(at_z((zl + d) % ZS)))
    for copy in copies[2:]:
        copy.start()
    ext2[...] = jnp.zeros_like(ext2)

    def remote(src, dst, ss, rs, device):
        return pltpu.make_async_remote_copy(
            src_ref=src, dst_ref=dst, send_sem=ss, recv_sem=rs,
            device_id=device, device_id_type=MESH,
        )

    copies[0].wait()
    rows = [ref[:, c, :] for ref in (u_ref, g_ref) for c in range(CHAN)]
    x = split(jnp.concatenate(rows, axis=0))
    y1 = dot3((first_ref[0], first_ref[1]), x, ((1,), (1,))).reshape(NCTX, 2, SLOTS, RADIX)
    copies[1].wait()
    sub = lax.broadcasted_iota(jnp.int32, (SLOTS, HALF), 0)
    keep = (lax.broadcasted_iota(jnp.int32, (NCTX, SLOTS, HALF), 0)
            + lax.broadcasted_iota(jnp.int32, (NCTX, SLOTS, HALF), 1)) > 0
    tc = turn_ref[0, :HALF].reshape(NCTX, SLOTS, HALF)
    ts = turn_ref[1, :HALF].reshape(NCTX, SLOTS, HALF)
    ec, es = turn_ref[0, HALF:], turn_ref[1, HALF:]
    extra = jnp.zeros((SLOTS, HALF), F32)
    for f in range(2):
        lanes = slice(f * HALF, (f + 1) * HALF)
        re = y1[:, 0, :, lanes]
        im = y1[:, 1, :, lanes]
        mid = jnp.broadcast_to(im[0, 0:1, :], (SLOTS, HALF))
        extra = jnp.where(sub == 2 * f, mid * ec, extra)
        extra = jnp.where(sub == 2 * f + 1, -mid * es, extra)
        im = jnp.where(keep, im, 0.0)
        send1[:, 2 * f] = re * tc + im * ts
        send1[:, 2 * f + 1] = im * tc - re * ts
    send1[SPECIAL, 4] = extra
    recv1[q, 0:4] = send1[q, 0:4]

    @pl.when(q == SPECIAL)
    def _():
        recv1[SPECIAL, 4] = send1[SPECIAL, 4]

    pl.semaphore_wait(barrier, NCTX - 1 + ((YS - 1 + 1 + ZS - 1) if full else 0))

    def tiles(special, count, act):
        @pl.when(special)
        def _():
            act(count + 1)

        @pl.when(jnp.logical_not(special))
        def _():
            act(count)

    def out1(p, count):
        return remote(
            send1.at[p, pl.ds(0, count)], recv1.at[q, pl.ds(0, count)], s1.at[p], r1.at[q], at_ctx(p))

    def in1(p, count):
        return remote(
            send1.at[p, pl.ds(0, count)], recv1.at[p, pl.ds(0, count)], s1.at[p], r1.at[p], at_ctx(p))

    def start1(d):
        p = (q + d) % NCTX
        tiles(p == SPECIAL, 4, lambda n: out1(p, n).start())

    each(NCTX, start1)
    for copy in copies[2:]:
        copy.wait()
    tiles(q == SPECIAL, 4, lambda n: each(NCTX, lambda d: in1((q + d) % NCTX, n).wait_recv()))

    def lane_ids(rows):
        return lax.broadcasted_iota(jnp.int32, (rows, HALF), 1)

    halves = [
        block_transpose([recv1[8 * h + j].reshape(40, HALF) for j in range(8)], lane_ids(40))
        for h in range(2)
    ]
    per_c = [jnp.concatenate([halves[0][c], halves[1][c]], axis=1) for c in range(CHAN)]
    for c in range(CHAN):
        ext[c] = per_c[c][32:40]
    planes = [per_c[c][8 * r : 8 * r + 8] for r in range(4) for c in range(CHAN)]
    planes += [ext[:, r, :] for r in range(4)]
    square = (square_ref[0], square_ref[1])
    spec = dot3(split(jnp.concatenate(planes, axis=0)), square)

    def forward(r):
        out = []
        for base, size in ((64 * r, 64), (256 + 8 * r, 8)):
            re, im = spec[base : base + size], spec[base + size : base + 2 * size]
            out.append((re[:, :RADIX] + im[:, RADIX:], im[:, :RADIX] - re[:, RADIX:]))
        return out

    us, gs = forward(0), forward(2)
    bc, bs = back_ref[0, :8], back_ref[1, :8]
    xc, xs = back_ref[0, 8:], back_ref[1, 8:]

    def out2(f, p, count):
        return remote(
            send2.at[f, p, pl.ds(0, count)], recv2.at[f, q, pl.ds(0, count)],
            s2.at[f, p], r2.at[f, q], at_ctx(p))

    def in2(f, p, count):
        return remote(
            send2.at[f, p, pl.ds(0, count)], recv2.at[f, p, pl.ds(0, count)],
            s2.at[f, p], r2.at[f, p], at_ctx(p))

    def inverse(f, main, side):
        inv = dot3(split(jnp.concatenate(main + side, axis=0)), square)
        re, im, xr, xi = inv[:64], inv[64:128], inv[128:136], inv[136:144]
        qr = (re[:, :RADIX] - im[:, RADIX:]).reshape(CHAN, SLOTS, RADIX)
        qi = (im[:, :RADIX] + re[:, RADIX:]).reshape(CHAN, SLOTS, RADIX)
        outs = (qr * bc[None] - qi * bs[None], qi * bc[None] + qr * bs[None])
        er = xr[:, :RADIX] - xi[:, RADIX:]
        ei = xi[:, :RADIX] + xr[:, RADIX:]
        ext2[f, :, 0, :] = er * xc - ei * xs
        per_c = [jnp.concatenate([outs[0][c], outs[1][c], ext2[f, c]], axis=0) for c in range(CHAN)]
        for h in range(2):
            parts = [v[:, h * HALF : (h + 1) * HALF] for v in per_c]
            for j, value in enumerate(block_transpose(parts, lane_ids(24))):
                send2[f, 8 * h + j] = value.reshape(3, SLOTS, HALF)
        recv2[f, q] = send2[f, q]
        tiles(q == SPECIAL, 2, lambda n: each(NCTX, lambda d: out2(f, (q + d) % NCTX, n).start()))

    def collect(f):
        def arrive(d):
            p = (q + d) % NCTX
            tiles(p == SPECIAL, 2, lambda n: in2(f, p, n).wait_recv())

        each(NCTX, arrive)
        recv2[f, 0, 1, 0:1, :] = recv2[f, SPECIAL, 2, 0:1, :]
        values = split(recv2[f, :, 0:2].reshape(RADIX, HALF))
        return dot3((last_ref[0], last_ref[1]), values).T

    corr = [
        [gr * ar + gi * ai, gi * ar - gr * ai]
        for (ar, ai), (gr, gi) in zip(us, gs)
    ]
    inverse(0, corr[0], corr[1])
    low = q < NCTX // 2
    hr = jnp.where(low, h_ref[0, :, 0:8, :], h_ref[0, :, 1:9, :]).reshape(64, RADIX)
    hi = jnp.where(low, h_ref[1, :, 0:8, :], h_ref[1, :, 1:9, :]).reshape(64, RADIX)
    hs = [(hr, hi), (h_ref[0, :, 0, :], h_ref[1, :, 0, :])]
    prod = [
        [fr * gr + fi * gi, fr * gi - fi * gr]
        for (fr, fi), (gr, gi) in zip(hs, gs)
    ]
    inverse(1, prod[0], prod[1])

    part[...] = collect(0).reshape(CHAN, COLS, HALF)

    def out_rs(yy):
        return remote(part.at[yy], gathered.at[y], rs_s.at[yy], rs_r.at[y], at_group(yy * 2 + core))

    def in_rs(yy):
        return remote(part.at[yy], gathered.at[yy], rs_s.at[yy], rs_r.at[yy], at_group(yy * 2 + core))

    if full:
        each(YS, lambda d: out_rs((y + d) % YS).start())
        gathered[y] = part[y]

    own = collect(1)
    for c in range(CHAN):
        in_out[:, c, :] = own[COLS * c : COLS * (c + 1)]

    if full:
        each(YS, lambda d: in_rs((y + d) % YS).wait_recv())
        zpart[zl] = jnp.sum(gathered[...], axis=0)

        def out_z(zz):
            return remote(zpart.at[zl], zpart.at[zl], z_s.at[zz], z_r.at[zl], at_z(zz))

        def in_z(zz):
            return remote(zpart.at[zz], zpart.at[zz], z_s.at[zz], z_r.at[zz], at_z(zz))

        each(ZS, lambda d: out_z((zl + d) % ZS).start())
        each(ZS, lambda d: in_z((zl + d) % ZS).wait_recv())
        everyone[core, y] = (zpart[0] + zpart[1]) + zpart[2]
        twin = at_group(m + 1 - 2 * core)

        def out_ag(yy):
            return remote(
                everyone.at[core, y], everyone.at[core, y], ag_s.at[yy], ag_r.at[y], at_group(yy * 2 + core))

        def in_ag(yy):
            return remote(
                everyone.at[core, yy], everyone.at[core, yy], ag_s.at[yy], ag_r.at[yy], at_group(yy * 2 + core))

        def out_twin(yy):
            return remote(everyone.at[core, yy], everyone.at[core, yy], c_s.at[yy], c_r.at[yy], twin)

        def in_twin(yy):
            return remote(everyone.at[1 - core, yy], everyone.at[1 - core, yy], c_s.at[yy], c_r.at[yy], twin)

        def near(d):
            return (y + jnp.where(d % 2 == 1, (d + 1) // 2, YS - d // 2)) % YS

        def hand_on(d):
            in_ag(near(d)).wait_recv()
            out_twin(near(d)).start()

        each(YS, lambda d: out_ag(near(YS - d)).start())
        out_twin(y).start()
        each(YS, hand_on)
        each(YS, lambda d: in_twin(near(d)).wait_recv())
        in_twin(y).wait_recv()
        for f in range(2 * CHAN):
            filt_out[:, f, :] = everyone[f // CHAN, f % CHAN]
        each(YS, lambda d: out_rs((y + d) % YS).wait_send())
        each(ZS, lambda d: out_z((zl + d) % ZS).wait_send())
        each(YS, lambda d: out_ag((y + d) % YS).wait_send())
        each(YS, lambda d: out_twin((y + d) % YS).wait_send())
        out_twin(y).wait_send()
    else:
        for f in range(2 * CHAN):
            filt_out[:, f, :] = part[f % CHAN]

    def finish1(d):
        p = (q + d) % NCTX
        tiles(p == SPECIAL, 4, lambda n: out1(p, n).wait_send())

    each(NCTX, finish1)
    for f in range(2):
        tiles(q == SPECIAL, 2, lambda n: each(NCTX, lambda d: out2(f, (q + d) % NCTX, n).wait_send()))


def body(saved_input, out_grad, filter_spec):
    full = lax.axis_size("ch") > 1
    first, turn, square, back, last = (jnp.asarray(t) for t in tables())
    vm = pl.BlockSpec(memory_space=pltpu.VMEM)
    hbm = pl.BlockSpec(memory_space=pltpu.HBM)
    sem = pltpu.SemaphoreType.DMA
    v = pltpu.VMEM
    return pl.pallas_call(
        functools.partial(kernel, full),
        out_shape=(
            jax.ShapeDtypeStruct((COLS, CHAN, HALF), F32),
            jax.ShapeDtypeStruct((COLS, 2 * CHAN, HALF), F32),
        ),
        in_specs=[vm] * 2 + [hbm] * 6,
        out_specs=(vm, vm),
        scratch_shapes=[
            v((2, RADIX, HALF), BF16),
            v((2, RADIX, 2 * RADIX), BF16),
            v((2, HALF, RADIX), BF16),
            v((2, CHAN, 16, RADIX), F32),
            v((2, HALF + 8, HALF), F32),
            v((2, 16, RADIX), F32),
            v((NCTX, 5, SLOTS, HALF), F32),
            v((NCTX, 5, SLOTS, HALF), F32),
            v((2, NCTX, 3, SLOTS, HALF), F32),
            v((2, NCTX, 3, SLOTS, HALF), F32),
            v((CHAN, 8, RADIX), F32),
            v((2, CHAN, 8, RADIX), F32),
            v((CHAN, COLS, HALF), F32),
            v((YS, COLS, HALF), F32),
            v((ZS, COLS, HALF), F32),
            v((2, CHAN, COLS, HALF), F32),
            sem((6,)),
            sem((NCTX,)), sem((NCTX,)), sem((2, NCTX)), sem((2, NCTX)),
            sem((YS,)), sem((YS,)), sem((ZS,)), sem((ZS,)),
            sem((YS,)), sem((YS,)), sem((YS,)), sem((YS,)),
        ],
        compiler_params=pltpu.CompilerParams(
            collective_id=0, has_side_effects=True, vmem_limit_bytes=56_229_888
        ),
        cost_estimate=pl.CostEstimate(flops=400_000_000, bytes_accessed=2_000_000, transcendentals=0),
    )(saved_input, out_grad, filter_spec, first, turn, square, back, last)


def solution(mesh):
    placed = (P("ctx", "ch", None), P("ctx", "ch", None), P(None, None, "ctx", None))
    return jax.shard_map(
        body,
        mesh=mesh,
        in_specs=placed,
        out_specs=(P("ctx", "ch", None), P("ctx", None, None)),
        check_vma=False,
    )
```

time: 71.3 us -> 63.7 us (0.89)
  local copies, waits for them, and re-layouts: 9.52 us -> 2.96 us
  Pallas kernels: 60.7 us -> 59.9 us
    unnamed x18 -> x6, local copies, waits for them, and re-layouts: 9.52 us -> 2.96 us
    pallas_call x1, Pallas kernels: 60.7 us -> 59.9 us  [body(): pl.pallas_call(functools.partial(kernel, full), out_shape=(jax.ShapeDtype...]
where the time goes in v2:
time: 63.7 us; the launch traced here: 63.5 us
  Pallas kernels  59.9 us (94%)
  local copies, waits for them, and re-layouts  2.96 us (5%)
  between operations  0.65 us (1%)
    pallas_call x1, Pallas kernels, body(): pl.pallas_call(functools.partial(kernel, full), out_shape=(jax.ShapeDtype...  59.9 us
    unnamed x6, local copies, waits for them, and re-layouts  2.96 us

profile of v2, /device:TPU:1, one launch (start us, length us, event | category | flops | bytes accessed | tf_op | source)
XLA Modules:
  0.0 63.5 jit_solution(2840854327038812827)
XLA Ops:
  0.6 0.0 copy-start
  0.6 0.8 %copy-done = f32[16,8,128]{2,1,0:T(8,128)S(1)} copy-done((f32[16,8,128]{2,1,0:T(8,128)S(1)}, f32[16,8,128]{2,1,0:T(8,128)}, u32[]{:S(2)}) %copy-start) | copy-done | bytes 65560
  1.5 0.0 copy-start.1
  1.5 0.8 %copy-done.1 = f32[16,8,128]{2,1,0:T(8,128)S(1)} copy-done((f32[16,8,128]{2,1,0:T(8,128)S(1)}, f32[16,8,128]{2,1,0:T(8,128)}, u32[]{:S(2)}) %copy-start.1) | copy-done | bytes 65560
  2.3 59.9 %shard_map.95 = (f32[16,8,128]{2,1,0:T(8,128)S(1)}, f32[16,16,128]{2,1,0:T(8,128)S(1)}) custom-call(f32[16,8,128]{2,1,0:T(8,128)S(1)} %copy-done, f32[16,8,128]{2,1,0:T(8,128)S(1)} %copy-done.1, f32[2,16,16,256]{3,2,1,0:T(8,128)} %h_hbm.1, bf16[2,256,128]{2,1,0:T(8,128)(2,1)} %constant.10.clone.first_hbm, f32[16,2,136,128]{3,2,1,0:T(8,128)} %constant.11.clone.turn_hbm, ...), custom_call_target="tpu_custom_call" | custom-call | flops 400000000 | bytes 2000000 | tf_op jit(solution)/shard_map/pallas_call | solution.py:383
  62.2 0.6 copy.12
  62.8 0.7 %copy.13 = f32[16,16,128]{2,1,0:T(8,128)} copy(f32[16,16,128]{2,1,0:T(8,128)S(1)} %get-tuple-element.5) | data formatting | bytes 262144
Async XLA Ops:
  0.6 0.8 %copy-start = (f32[16,8,128]{2,1,0:T(8,128)S(1)}, f32[16,8,128]{2,1,0:T(8,128)}, u32[]{:S(2)}) copy-start(f32[16,8,128]{2,1,0:T(8,128)} %u_ref.1) | copy-start | bytes 196612
  1.5 0.8 %copy-start.1 = (f32[16,8,128]{2,1,0:T(8,128)S(1)}, f32[16,8,128]{2,1,0:T(8,128)}, u32[]{:S(2)}) copy-start(f32[16,8,128]{2,1,0:T(8,128)} %g_ref.1) | copy-start | bytes 196612

commit v3 on v2

--- a/solution.py
+++ b/solution.py
@@ -99,7 +99,7 @@
 
 def kernel(
     full,
-    u_ref, g_ref, h_hbm, first_hbm, turn_hbm, square_hbm, back_hbm, last_hbm,
+    field_ref, h_hbm, first_hbm, turn_hbm, square_hbm, back_hbm, last_hbm,
     in_out, filt_out,
     first_ref, square_ref, last_ref,
     h_ref, turn_ref, back_ref, send1, recv1, send2, recv2, ext, ext2,
@@ -162,7 +162,7 @@
         )
 
     copies[0].wait()
-    rows = [ref[:, c, :] for ref in (u_ref, g_ref) for c in range(CHAN)]
+    rows = [field_ref[f, :, c, :] for f in range(2) for c in range(CHAN)]
     x = split(jnp.concatenate(rows, axis=0))
     y1 = dot3((first_ref[0], first_ref[1]), x, ((1,), (1,))).reshape(NCTX, 2, SLOTS, RADIX)
     copies[1].wait()
@@ -216,22 +216,33 @@
     each(NCTX, start1)
     for copy in copies[2:]:
         copy.wait()
-    tiles(q == SPECIAL, 4, lambda n: each(NCTX, lambda d: in1((q + d) % NCTX, n).wait_recv()))
 
     def lane_ids(rows):
         return lax.broadcasted_iota(jnp.int32, (rows, HALF), 1)
 
-    halves = [
-        block_transpose([recv1[8 * h + j].reshape(40, HALF) for j in range(8)], lane_ids(40))
-        for h in range(2)
-    ]
-    per_c = [jnp.concatenate([halves[0][c], halves[1][c]], axis=1) for c in range(CHAN)]
-    for c in range(CHAN):
-        ext[c] = per_c[c][32:40]
-    planes = [per_c[c][8 * r : 8 * r + 8] for r in range(4) for c in range(CHAN)]
-    planes += [ext[:, r, :] for r in range(4)]
     square = (square_ref[0], square_ref[1])
-    spec = dot3(split(jnp.concatenate(planes, axis=0)), square)
+
+    def partial(h):
+        def arrive(j):
+            p = 8 * h + j
+
+            @pl.when(p != q)
+            def _():
+                tiles(q == SPECIAL, 4, lambda n: in1(p, n).wait_recv())
+
+        lax.fori_loop(0, 8, lambda j, carry: (arrive(j), carry)[1], 0)
+        per_c = block_transpose(
+            [recv1[8 * h + j].reshape(40, HALF) for j in range(8)], lane_ids(40))
+        for c in range(CHAN):
+            ext[c] = per_c[c][32:40]
+        planes = [per_c[c][8 * r : 8 * r + 8] for r in range(4) for c in range(CHAN)]
+        planes += [ext[:, r, :] for r in range(4)]
+        rows = pl.ds(pl.multiple_of(h * HALF, HALF), HALF)
+        return dot3(split(jnp.concatenate(planes, axis=0)), (square_ref[0, rows, :], square_ref[1, rows, :]))
+
+    own_half = q // 8
+    spec = partial(own_half)
+    spec = spec + partial(1 - own_half)
 
     def forward(r):
         out = []
@@ -268,8 +279,8 @@
             parts = [v[:, h * HALF : (h + 1) * HALF] for v in per_c]
             for j, value in enumerate(block_transpose(parts, lane_ids(24))):
                 send2[f, 8 * h + j] = value.reshape(3, SLOTS, HALF)
+        tiles(q == SPECIAL, 2, lambda n: each(NCTX, lambda d: out2(f, (q + d) % NCTX, n).start()))
         recv2[f, q] = send2[f, q]
-        tiles(q == SPECIAL, 2, lambda n: each(NCTX, lambda d: out2(f, (q + d) % NCTX, n).start()))
 
     def collect(f):
         def arrive(d):
@@ -298,6 +309,9 @@
 
     part[...] = collect(0).reshape(CHAN, COLS, HALF)
 
+    def near(d):
+        return (y + jnp.where(d % 2 == 1, (d + 1) // 2, YS - d // 2)) % YS
+
     def out_rs(yy):
         return remote(part.at[yy], gathered.at[y], rs_s.at[yy], rs_r.at[y], at_group(yy * 2 + core))
 
@@ -305,7 +319,7 @@
         return remote(part.at[yy], gathered.at[yy], rs_s.at[yy], rs_r.at[yy], at_group(yy * 2 + core))
 
     if full:
-        each(YS, lambda d: out_rs((y + d) % YS).start())
+        each(YS, lambda d: out_rs(near(YS - d)).start())
         gathered[y] = part[y]
 
     own = collect(1)
@@ -313,7 +327,7 @@
         in_out[:, c, :] = own[COLS * c : COLS * (c + 1)]
 
     if full:
-        each(YS, lambda d: in_rs((y + d) % YS).wait_recv())
+        each(YS, lambda d: in_rs(near(d)).wait_recv())
         zpart[zl] = jnp.sum(gathered[...], axis=0)
 
         def out_z(zz):
@@ -341,9 +355,6 @@
         def in_twin(yy):
             return remote(everyone.at[1 - core, yy], everyone.at[1 - core, yy], c_s.at[yy], c_r.at[yy], twin)
 
-        def near(d):
-            return (y + jnp.where(d % 2 == 1, (d + 1) // 2, YS - d // 2)) % YS
-
         def hand_on(d):
             in_ag(near(d)).wait_recv()
             out_twin(near(d)).start()
@@ -351,10 +362,22 @@
         each(YS, lambda d: out_ag(near(YS - d)).start())
         out_twin(y).start()
         each(YS, hand_on)
+
+        def place(which):
+            @pl.when(which == 0)
+            def _():
+                for f in range(CHAN):
+                    filt_out[:, f, :] = everyone[0, f]
+
+            @pl.when(which == 1)
+            def _():
+                for f in range(CHAN):
+                    filt_out[:, CHAN + f, :] = everyone[1, f]
+
+        place(core)
+        in_twin(y).wait_recv()
         each(YS, lambda d: in_twin(near(d)).wait_recv())
-        in_twin(y).wait_recv()
-        for f in range(2 * CHAN):
-            filt_out[:, f, :] = everyone[f // CHAN, f % CHAN]
+        place(1 - core)
         each(YS, lambda d: out_rs((y + d) % YS).wait_send())
         each(ZS, lambda d: out_z((zl + d) % ZS).wait_send())
         each(YS, lambda d: out_ag((y + d) % YS).wait_send())
@@ -386,7 +409,7 @@
             jax.ShapeDtypeStruct((COLS, CHAN, HALF), F32),
             jax.ShapeDtypeStruct((COLS, 2 * CHAN, HALF), F32),
         ),
-        in_specs=[vm] * 2 + [hbm] * 6,
+        in_specs=[vm] + [hbm] * 6,
         out_specs=(vm, vm),
         scratch_shapes=[
             v((2, RADIX, HALF), BF16),
@@ -399,7 +422,7 @@
             v((NCTX, 5, SLOTS, HALF), F32),
             v((2, NCTX, 3, SLOTS, HALF), F32),
             v((2, NCTX, 3, SLOTS, HALF), F32),
-            v((CHAN, 8, RADIX), F32),
+            v((CHAN, 8, HALF), F32),
             v((2, CHAN, 8, RADIX), F32),
             v((CHAN, COLS, HALF), F32),
             v((YS, COLS, HALF), F32),
@@ -414,7 +437,7 @@
             collective_id=0, has_side_effects=True, vmem_limit_bytes=56_229_888
         ),
         cost_estimate=pl.CostEstimate(flops=400_000_000, bytes_accessed=2_000_000, transcendentals=0),
-    )(saved_input, out_grad, filter_spec, first, turn, square, back, last)
+    )(jnp.stack([saved_input, out_grad]), filter_spec, first, turn, square, back, last)
 
 
 def solution(mesh):

time: 63.7 us -> 63.4 us (level)
  local copies, waits for them, and re-layouts: 2.96 us -> 1.29 us
  other arithmetic: 0 us -> 0.88 us
    unnamed x6 -> x2, local copies, waits for them, and re-layouts: 2.96 us -> 1.29 us
    another operation x0 -> x1, other arithmetic: none -> 0.88 us  [body(): jnp.stack([saved_input, out_grad])]
where the time goes in v3:
time: 63.4 us; the launch traced here: 63.2 us
  Pallas kernels  60.4 us (95%)
  local copies, waits for them, and re-layouts  1.29 us (2%)
  other arithmetic  0.88 us (1%)
  between operations  0.64 us (1%)
    pallas_call x1, Pallas kernels, body(): pl.pallas_call(functools.partial(kernel, full), out_shape=(jax.ShapeDtype...  60.4 us
    unnamed x2, local copies, waits for them, and re-layouts  1.29 us

profile of v3, /device:TPU:1, one launch (start us, length us, event | category | flops | bytes accessed | tf_op | source)
XLA Modules:
  0.0 63.2 jit_solution(2269762346193458103)
XLA Ops:
  0.6 0.9 %pad_maximum_fusion.field_ref = f32[2,16,8,128]{3,2,1,0:T(8,128)S(1)} fusion(f32[1,16,8,128]{3,2,1,0:T(8,128)} %bitcast.2, f32[1,16,8,128]{3,2,1,0:T(8,128)} %bitcast.3), kind=kLoop, calls=%fused_computation | loop fusion | flops 32768 | bytes 262144 | tf_op jit(solution)/shard_map/stack | solution.py:440
  1.5 60.4 %shard_map.95 = (f32[16,8,128]{2,1,0:T(8,128)S(1)}, f32[16,16,128]{2,1,0:T(8,128)S(1)}) custom-call(f32[2,16,8,128]{3,2,1,0:T(8,128)S(1)} %pad_maximum_fusion.field_ref, f32[2,16,16,256]{3,2,1,0:T(8,128)} %h_hbm.1, bf16[2,256,128]{2,1,0:T(8,128)(2,1)} %constant.10.clone.first_hbm, f32[16,2,136,128]{3,2,1,0:T(8,128)} %constant.11.clone.turn_hbm, ...), custom_call_target="tpu_custom_call" | custom-call | flops 400000000 | bytes 2000000 | tf_op jit(solution)/shard_map/pallas_call | solution.py:406
  61.9 0.6 copy.12
  62.6 0.7 %copy.13 = f32[16,16,128]{2,1,0:T(8,128)} copy(f32[16,16,128]{2,1,0:T(8,128)S(1)} %get-tuple-element.5) | data formatting | bytes 262144

commit v4 on v3

--- a/solution.py
+++ b/solution.py
@@ -26,10 +26,10 @@
 BF16 = jnp.bfloat16
 
 
-def split_np(table):
+def split_np(table, axis, order):
     high = table.astype(np.float32).astype(ml_dtypes.bfloat16)
     low = (table - high.astype(np.float64)).astype(np.float32).astype(ml_dtypes.bfloat16)
-    return np.stack([high, low])
+    return np.concatenate([(high, low)[part] for part in order], axis=axis)
 
 
 def slot_freqs():
@@ -50,14 +50,14 @@
     ang = angle(k1[:, :, None] * a[None, None, :], RADIX)
     first = np.stack([np.cos(ang), -np.sin(ang)], axis=1)
     first[0, 1, 0] = alt
-    first = split_np(first.reshape(RADIX, HALF))
+    first = split_np(first.reshape(RADIX, HALF), 1, (0, 1, 0))
     weight = np.full((NCTX, SLOTS, 1), 2.0)
     weight[0, 0] = 1.0
     last = np.stack([weight * np.cos(ang), -weight * np.sin(ang)], axis=1)
     last[0, 1, 0] = alt
-    last = split_np(np.ascontiguousarray(last.reshape(RADIX, HALF).T) / PADDED)
+    last = split_np(last.reshape(RADIX, HALF).T / PADDED, 1, (0, 1, 0))
     both = angle(b[:, None] * b[None, :], RADIX)
-    square = split_np(np.concatenate([np.cos(both), np.sin(both)], axis=1))
+    square = split_np(np.concatenate([np.cos(both), np.sin(both)], axis=1), 0, (0, 0, 1))
     bp = b.reshape(NCTX, COLS)
     lanes = np.tile(bp, (1, CHAN))
     rows = np.concatenate([k1.reshape(-1), np.full(8, HALF)])
@@ -69,18 +69,14 @@
     return first, turn, square, back, last
 
 
-def split(values):
+def split(values, axis, order):
     high = values.astype(BF16)
     low = (values - high.astype(F32)).astype(BF16)
-    return high, low
+    return jnp.concatenate([(high, low)[part] for part in order], axis=axis)
 
 
 def dot(x, y, dims=((1,), (0,))):
     return lax.dot_general(x, y, (dims, ((), ())), preferred_element_type=F32)
-
-
-def dot3(x, y, dims=((1,), (0,))):
-    return dot(x[0], y[0], dims) + (dot(x[1], y[0], dims) + dot(x[0], y[1], dims))
 
 
 def block_transpose(parts, lane):
@@ -144,11 +140,17 @@
             fn(d)
             return carry
 
-        lax.fori_loop(1, count, step, 0)
-
-    each(NCTX, lambda d: greet(at_ctx((q + d) % NCTX)))
+        lax.fori_loop(1, count, step, 0, unroll=True)
+
+    def gray(n):
+        return n ^ (n >> 1)
+
+    def far(d):
+        return q ^ (4 * gray(3 - ((d - 1) & 3)) + gray(3 - ((d - 1) >> 2)))
+
+    each(NCTX, lambda d: greet(at_ctx(far(d))))
     if full:
-        each(YS, lambda d: greet(at_group((y + d) % YS * 2 + core)))
+        each(YS, lambda d: greet(at_group(((y + d) & (YS - 1)) * 2 + core)))
         greet(at_group(m + 1 - 2 * core))
         each(ZS, lambda d: greet(at_z((zl + d) % ZS)))
     for copy in copies[2:]:
@@ -163,8 +165,8 @@
 
     copies[0].wait()
     rows = [field_ref[f, :, c, :] for f in range(2) for c in range(CHAN)]
-    x = split(jnp.concatenate(rows, axis=0))
-    y1 = dot3((first_ref[0], first_ref[1]), x, ((1,), (1,))).reshape(NCTX, 2, SLOTS, RADIX)
+    x = split(jnp.concatenate(rows, axis=0), 1, (0, 0, 1))
+    y1 = dot(first_ref[...], x, ((1,), (1,))).reshape(NCTX, 2, SLOTS, RADIX)
     copies[1].wait()
     sub = lax.broadcasted_iota(jnp.int32, (SLOTS, HALF), 0)
     keep = (lax.broadcasted_iota(jnp.int32, (NCTX, SLOTS, HALF), 0)
@@ -210,39 +212,28 @@
             send1.at[p, pl.ds(0, count)], recv1.at[p, pl.ds(0, count)], s1.at[p], r1.at[p], at_ctx(p))
 
     def start1(d):
-        p = (q + d) % NCTX
+        p = far(d)
         tiles(p == SPECIAL, 4, lambda n: out1(p, n).start())
 
     each(NCTX, start1)
     for copy in copies[2:]:
         copy.wait()
+    tiles(q == SPECIAL, 4, lambda n: each(NCTX, lambda d: in1(((q + d) & (NCTX - 1)), n).wait_recv()))
 
     def lane_ids(rows):
         return lax.broadcasted_iota(jnp.int32, (rows, HALF), 1)
 
-    square = (square_ref[0], square_ref[1])
-
-    def partial(h):
-        def arrive(j):
-            p = 8 * h + j
-
-            @pl.when(p != q)
-            def _():
-                tiles(q == SPECIAL, 4, lambda n: in1(p, n).wait_recv())
-
-        lax.fori_loop(0, 8, lambda j, carry: (arrive(j), carry)[1], 0)
-        per_c = block_transpose(
-            [recv1[8 * h + j].reshape(40, HALF) for j in range(8)], lane_ids(40))
-        for c in range(CHAN):
-            ext[c] = per_c[c][32:40]
-        planes = [per_c[c][8 * r : 8 * r + 8] for r in range(4) for c in range(CHAN)]
-        planes += [ext[:, r, :] for r in range(4)]
-        rows = pl.ds(pl.multiple_of(h * HALF, HALF), HALF)
-        return dot3(split(jnp.concatenate(planes, axis=0)), (square_ref[0, rows, :], square_ref[1, rows, :]))
-
-    own_half = q // 8
-    spec = partial(own_half)
-    spec = spec + partial(1 - own_half)
+    halves = [
+        block_transpose([recv1[8 * h + j].reshape(40, HALF) for j in range(8)], lane_ids(40))
+        for h in range(2)
+    ]
+    per_c = [jnp.concatenate([halves[0][c], halves[1][c]], axis=1) for c in range(CHAN)]
+    for c in range(CHAN):
+        ext[c] = per_c[c][32:40]
+    planes = [per_c[c][8 * r : 8 * r + 8] for r in range(4) for c in range(CHAN)]
+    planes += [ext[:, r, :] for r in range(4)]
+    square = square_ref[...]
+    spec = dot(split(jnp.concatenate(planes, axis=0), 1, (0, 1, 0)), square)
 
     def forward(r):
         out = []
@@ -266,7 +257,7 @@
             s2.at[f, p], r2.at[f, p], at_ctx(p))
 
     def inverse(f, main, side):
-        inv = dot3(split(jnp.concatenate(main + side, axis=0)), square)
+        inv = dot(split(jnp.concatenate(main + side, axis=0), 1, (0, 1, 0)), square)
         re, im, xr, xi = inv[:64], inv[64:128], inv[128:136], inv[136:144]
         qr = (re[:, :RADIX] - im[:, RADIX:]).reshape(CHAN, SLOTS, RADIX)
         qi = (im[:, :RADIX] + re[:, RADIX:]).reshape(CHAN, SLOTS, RADIX)
@@ -279,24 +270,28 @@
             parts = [v[:, h * HALF : (h + 1) * HALF] for v in per_c]
             for j, value in enumerate(block_transpose(parts, lane_ids(24))):
                 send2[f, 8 * h + j] = value.reshape(3, SLOTS, HALF)
-        tiles(q == SPECIAL, 2, lambda n: each(NCTX, lambda d: out2(f, (q + d) % NCTX, n).start()))
         recv2[f, q] = send2[f, q]
+
+    def leave(f):
+        tiles(q == SPECIAL, 2, lambda n: each(NCTX, lambda d: out2(f, far(d), n).start()))
+
 
     def collect(f):
         def arrive(d):
-            p = (q + d) % NCTX
+            p = ((q + d) & (NCTX - 1))
             tiles(p == SPECIAL, 2, lambda n: in2(f, p, n).wait_recv())
 
         each(NCTX, arrive)
         recv2[f, 0, 1, 0:1, :] = recv2[f, SPECIAL, 2, 0:1, :]
-        values = split(recv2[f, :, 0:2].reshape(RADIX, HALF))
-        return dot3((last_ref[0], last_ref[1]), values).T
+        values = split(recv2[f, :, 0:2].reshape(RADIX, HALF), 0, (0, 0, 1))
+        return dot(last_ref[...], values).T
 
     corr = [
         [gr * ar + gi * ai, gi * ar - gr * ai]
         for (ar, ai), (gr, gi) in zip(us, gs)
     ]
     inverse(0, corr[0], corr[1])
+    leave(0)
     low = q < NCTX // 2
     hr = jnp.where(low, h_ref[0, :, 0:8, :], h_ref[0, :, 1:9, :]).reshape(64, RADIX)
     hi = jnp.where(low, h_ref[1, :, 0:8, :], h_ref[1, :, 1:9, :]).reshape(64, RADIX)
@@ -310,7 +305,7 @@
     part[...] = collect(0).reshape(CHAN, COLS, HALF)
 
     def near(d):
-        return (y + jnp.where(d % 2 == 1, (d + 1) // 2, YS - d // 2)) % YS
+        return (y + jnp.where((d & 1) == 1, (d + 1) >> 1, YS - (d >> 1))) & (YS - 1)
 
     def out_rs(yy):
         return remote(part.at[yy], gathered.at[y], rs_s.at[yy], rs_r.at[y], at_group(yy * 2 + core))
@@ -322,9 +317,7 @@
         each(YS, lambda d: out_rs(near(YS - d)).start())
         gathered[y] = part[y]
 
-    own = collect(1)
-    for c in range(CHAN):
-        in_out[:, c, :] = own[COLS * c : COLS * (c + 1)]
+    leave(1)
 
     if full:
         each(YS, lambda d: in_rs(near(d)).wait_recv())
@@ -361,6 +354,9 @@
 
         each(YS, lambda d: out_ag(near(YS - d)).start())
         out_twin(y).start()
+        own = collect(1)
+        for c in range(CHAN):
+            in_out[:, c, :] = own[COLS * c : COLS * (c + 1)]
         each(YS, hand_on)
 
         def place(which):
@@ -378,22 +374,25 @@
         in_twin(y).wait_recv()
         each(YS, lambda d: in_twin(near(d)).wait_recv())
         place(1 - core)
-        each(YS, lambda d: out_rs((y + d) % YS).wait_send())
+        each(YS, lambda d: out_rs(((y + d) & (YS - 1))).wait_send())
         each(ZS, lambda d: out_z((zl + d) % ZS).wait_send())
-        each(YS, lambda d: out_ag((y + d) % YS).wait_send())
-        each(YS, lambda d: out_twin((y + d) % YS).wait_send())
+        each(YS, lambda d: out_ag(((y + d) & (YS - 1))).wait_send())
+        each(YS, lambda d: out_twin(((y + d) & (YS - 1))).wait_send())
         out_twin(y).wait_send()
     else:
+        own = collect(1)
+        for c in range(CHAN):
+            in_out[:, c, :] = own[COLS * c : COLS * (c + 1)]
         for f in range(2 * CHAN):
             filt_out[:, f, :] = part[f % CHAN]
 
     def finish1(d):
-        p = (q + d) % NCTX
+        p = ((q + d) & (NCTX - 1))
         tiles(p == SPECIAL, 4, lambda n: out1(p, n).wait_send())
 
     each(NCTX, finish1)
     for f in range(2):
-        tiles(q == SPECIAL, 2, lambda n: each(NCTX, lambda d: out2(f, (q + d) % NCTX, n).wait_send()))
+        tiles(q == SPECIAL, 2, lambda n: each(NCTX, lambda d: out2(f, ((q + d) & (NCTX - 1)), n).wait_send()))
 
 
 def body(saved_input, out_grad, filter_spec):
@@ -412,9 +411,9 @@
         in_specs=[vm] + [hbm] * 6,
         out_specs=(vm, vm),
         scratch_shapes=[
-            v((2, RADIX, HALF), BF16),
-            v((2, RADIX, 2 * RADIX), BF16),
-            v((2, HALF, RADIX), BF16),
+            v((RADIX, 3 * HALF), BF16),
+            v((3 * RADIX, 2 * RADIX), BF16),
+            v((HALF, 3 * RADIX), BF16),
             v((2, CHAN, 16, RADIX), F32),
             v((2, HALF + 8, HALF), F32),
             v((2, 16, RADIX), F32),
@@ -422,7 +421,7 @@
             v((NCTX, 5, SLOTS, HALF), F32),
             v((2, NCTX, 3, SLOTS, HALF), F32),
             v((2, NCTX, 3, SLOTS, HALF), F32),
-            v((CHAN, 8, HALF), F32),
+            v((CHAN, 8, RADIX), F32),
             v((2, CHAN, 8, RADIX), F32),
             v((CHAN, COLS, HALF), F32),
             v((YS, COLS, HALF), F32),

time: 63.4 us -> 58.3 us (0.920)
  Pallas kernels: 60.4 us -> 55.2 us
    pallas_call x1, Pallas kernels: 60.4 us -> 55.2 us  [body(): pl.pallas_call(functools.partial(kernel, full), out_shape=(jax.ShapeDtype...]
where the time goes in v4:
time: 58.3 us; the launch traced here: 58.1 us
  Pallas kernels  55.2 us (95%)
  local copies, waits for them, and re-layouts  1.29 us (2%)
  other arithmetic  0.88 us (2%)
  between operations  0.64 us (1%)
    pallas_call x1, Pallas kernels, body(): pl.pallas_call(functools.partial(kernel, full), out_shape=(jax.ShapeDtype...  55.2 us
    unnamed x2, local copies, waits for them, and re-layouts  1.29 us

profile of v4, /device:TPU:1, one launch (start us, length us, event | category | flops | bytes accessed | tf_op | source)
XLA Modules:
  0.0 58.1 jit_solution(8312401586170363666)
XLA Ops:
  0.6 0.9 %pad_maximum_fusion.field_ref = f32[2,16,8,128]{3,2,1,0:T(8,128)S(1)} fusion(f32[1,16,8,128]{3,2,1,0:T(8,128)} %bitcast.2, f32[1,16,8,128]{3,2,1,0:T(8,128)} %bitcast.3), kind=kLoop, calls=%fused_computation | loop fusion | flops 32768 | bytes 262144 | tf_op jit(solution)/shard_map/stack | solution.py:439
  1.5 55.2 %shard_map.95 = (f32[16,8,128]{2,1,0:T(8,128)S(1)}, f32[16,16,128]{2,1,0:T(8,128)S(1)}) custom-call(f32[2,16,8,128]{3,2,1,0:T(8,128)S(1)} %pad_maximum_fusion.field_ref, f32[2,16,16,256]{3,2,1,0:T(8,128)} %h_hbm.1, bf16[256,384]{1,0:T(8,128)(2,1)} %constant.10.clone.first_hbm, f32[16,2,136,128]{3,2,1,0:T(8,128)} %constant.11.clone.turn_hbm, ...), custom_call_target="tpu_custom_call" | custom-call | flops 400000000 | bytes 2000000 | tf_op jit(solution)/shard_map/pallas_call | solution.py:405
  56.8 0.6 %copy.12 = f32[16,8,128]{2,1,0:T(8,128)} copy(f32[16,8,128]{2,1,0:T(8,128)S(1)} %get-tuple-element.4) | data formatting | bytes 131072
  57.4 0.7 %copy.13 = f32[16,16,128]{2,1,0:T(8,128)} copy(f32[16,16,128]{2,1,0:T(8,128)S(1)} %get-tuple-element.5) | data formatting | bytes 262144

commit v5 on v4

--- a/solution.py
+++ b/solution.py
@@ -146,7 +146,11 @@
         return n ^ (n >> 1)
 
     def far(d):
-        return q ^ (4 * gray(3 - ((d - 1) & 3)) + gray(3 - ((d - 1) >> 2)))
+        i = d - 1
+        mixed = (i >= 4) & (i < 12)
+        xi = jnp.where(mixed, (i - 4) >> 1, i & 3)
+        zz = jnp.where(mixed, 3 - 2 * (i & 1), jnp.where(i < 4, 2, 0))
+        return q ^ (4 * gray(3 - xi) + zz)
 
     each(NCTX, lambda d: greet(at_ctx(far(d))))
     if full:

time: 58.3 us -> 58.3 us (level)
  no operation moved by 1% of the time
where the time goes in v5:
time: 58.3 us; the launch traced here: 58.2 us
  Pallas kernels  55.3 us (95%)
  local copies, waits for them, and re-layouts  1.29 us (2%)
  other arithmetic  0.88 us (2%)
  between operations  0.64 us (1%)
    pallas_call x1, Pallas kernels, body(): pl.pallas_call(functools.partial(kernel, full), out_shape=(jax.ShapeDtype...  55.3 us
    unnamed x2, local copies, waits for them, and re-layouts  1.29 us

profile of v5, /device:TPU:1, one launch (start us, length us, event | category | flops | bytes accessed | tf_op | source)
XLA Modules:
  0.0 58.2 jit_solution(1556568443477996601)
XLA Ops:
  0.6 0.9 %pad_maximum_fusion.field_ref = f32[2,16,8,128]{3,2,1,0:T(8,128)S(1)} fusion(f32[1,16,8,128]{3,2,1,0:T(8,128)} %bitcast.2, f32[1,16,8,128]{3,2,1,0:T(8,128)} %bitcast.3), kind=kLoop, calls=%fused_computation | loop fusion | flops 32768 | bytes 262144 | tf_op jit(solution)/shard_map/stack | solution.py:443
  1.5 55.3 %shard_map.95 = (f32[16,8,128]{2,1,0:T(8,128)S(1)}, f32[16,16,128]{2,1,0:T(8,128)S(1)}) custom-call(f32[2,16,8,128]{3,2,1,0:T(8,128)S(1)} %pad_maximum_fusion.field_ref, f32[2,16,16,256]{3,2,1,0:T(8,128)} %h_hbm.1, bf16[256,384]{1,0:T(8,128)(2,1)} %constant.10.clone.first_hbm, f32[16,2,136,128]{3,2,1,0:T(8,128)} %constant.11.clone.turn_hbm, ...), custom_call_target="tpu_custom_call" | custom-call | flops 400000000 | bytes 2000000 | tf_op jit(solution)/shard_map/pallas_call | solution.py:409
  56.9 0.6 %copy.12 = f32[16,8,128]{2,1,0:T(8,128)} copy(f32[16,8,128]{2,1,0:T(8,128)S(1)} %get-tuple-element.4) | data formatting | bytes 131072
  57.5 0.7 %copy.13 = f32[16,16,128]{2,1,0:T(8,128)} copy(f32[16,16,128]{2,1,0:T(8,128)S(1)} %get-tuple-element.5) | data formatting | bytes 262144

commit v6 on v5

--- a/solution.py
+++ b/solution.py
@@ -21,6 +21,7 @@
 YS = 8
 GROUP = 16
 ZS = 3
+TRIPLE = 24
 SPECIAL = 8
 F32 = jnp.float32
 BF16 = jnp.bfloat16
@@ -99,8 +100,8 @@
     in_out, filt_out,
     first_ref, square_ref, last_ref,
     h_ref, turn_ref, back_ref, send1, recv1, send2, recv2, ext, ext2,
-    part, gathered, zpart, everyone,
-    local_sem, s1, r1, s2, r2, rs_s, rs_r, z_s, z_r, ag_s, ag_r, c_s, c_r,
+    part, gathered, everyone,
+    local_sem, s1, r1, s2, r2, rs_s, rs_r, ag_s, ag_r, c_s, c_r,
 ):
     q = lax.axis_index("ctx")
     ch = lax.axis_index("ch")
@@ -129,8 +130,10 @@
     def at_group(mm):
         return (q, zl * GROUP + mm)
 
-    def at_z(zz):
-        return (q, zz * GROUP + m)
+    me = zl * YS + y
+
+    def at_triple(t):
+        return (q, (t // YS) * GROUP + (t % YS) * 2 + core)
 
     def greet(device):
         pl.semaphore_signal(barrier, inc=1, device_id=device, device_id_type=MESH)
@@ -154,9 +157,8 @@
 
     each(NCTX, lambda d: greet(at_ctx(far(d))))
     if full:
-        each(YS, lambda d: greet(at_group(((y + d) & (YS - 1)) * 2 + core)))
+        each(TRIPLE, lambda d: greet(at_triple((me + d) % TRIPLE)))
         greet(at_group(m + 1 - 2 * core))
-        each(ZS, lambda d: greet(at_z((zl + d) % ZS)))
     for copy in copies[2:]:
         copy.start()
     ext2[...] = jnp.zeros_like(ext2)
@@ -196,7 +198,7 @@
     def _():
         recv1[SPECIAL, 4] = send1[SPECIAL, 4]
 
-    pl.semaphore_wait(barrier, NCTX - 1 + ((YS - 1 + 1 + ZS - 1) if full else 0))
+    pl.semaphore_wait(barrier, NCTX - 1 + (TRIPLE if full else 0))
 
     def tiles(special, count, act):
         @pl.when(special)
@@ -311,31 +313,25 @@
     def near(d):
         return (y + jnp.where((d & 1) == 1, (d + 1) >> 1, YS - (d >> 1))) & (YS - 1)
 
-    def out_rs(yy):
-        return remote(part.at[yy], gathered.at[y], rs_s.at[yy], rs_r.at[y], at_group(yy * 2 + core))
-
-    def in_rs(yy):
-        return remote(part.at[yy], gathered.at[yy], rs_s.at[yy], rs_r.at[yy], at_group(yy * 2 + core))
+    def out_rs(t):
+        return remote(part.at[t % YS], gathered.at[me], rs_s.at[t], rs_r.at[me], at_triple(t))
+
+    def in_rs(t):
+        return remote(part.at[t % YS], gathered.at[t], rs_s.at[t], rs_r.at[t], at_triple(t))
 
     if full:
-        each(YS, lambda d: out_rs(near(YS - d)).start())
-        gathered[y] = part[y]
+        for dz in (1, 2):
+            other = (zl + dz) % ZS * YS
+            each(YS, lambda d: out_rs(other + near(YS - d)).start())
+            out_rs(other + y).start()
+        each(YS, lambda d: out_rs(zl * YS + near(YS - d)).start())
+        gathered[me] = part[y]
 
     leave(1)
 
     if full:
-        each(YS, lambda d: in_rs(near(d)).wait_recv())
-        zpart[zl] = jnp.sum(gathered[...], axis=0)
-
-        def out_z(zz):
-            return remote(zpart.at[zl], zpart.at[zl], z_s.at[zz], z_r.at[zl], at_z(zz))
-
-        def in_z(zz):
-            return remote(zpart.at[zz], zpart.at[zz], z_s.at[zz], z_r.at[zz], at_z(zz))
-
-        each(ZS, lambda d: out_z((zl + d) % ZS).start())
-        each(ZS, lambda d: in_z((zl + d) % ZS).wait_recv())
-        everyone[core, y] = (zpart[0] + zpart[1]) + zpart[2]
+        each(TRIPLE, lambda d: in_rs((me + d) % TRIPLE).wait_recv())
+        everyone[core, y] = jnp.sum(gathered[...], axis=0)
         twin = at_group(m + 1 - 2 * core)
 
         def out_ag(yy):
@@ -378,8 +374,7 @@
         in_twin(y).wait_recv()
         each(YS, lambda d: in_twin(near(d)).wait_recv())
         place(1 - core)
-        each(YS, lambda d: out_rs(((y + d) & (YS - 1))).wait_send())
-        each(ZS, lambda d: out_z((zl + d) % ZS).wait_send())
+        each(TRIPLE, lambda d: out_rs((me + d) % TRIPLE).wait_send())
         each(YS, lambda d: out_ag(((y + d) & (YS - 1))).wait_send())
         each(YS, lambda d: out_twin(((y + d) & (YS - 1))).wait_send())
         out_twin(y).wait_send()
@@ -428,12 +423,11 @@
             v((CHAN, 8, RADIX), F32),
             v((2, CHAN, 8, RADIX), F32),
             v((CHAN, COLS, HALF), F32),
-            v((YS, COLS, HALF), F32),
-            v((ZS, COLS, HALF), F32),
+            v((TRIPLE, COLS, HALF), F32),
             v((2, CHAN, COLS, HALF), F32),
             sem((6,)),
             sem((NCTX,)), sem((NCTX,)), sem((2, NCTX)), sem((2, NCTX)),
-            sem((YS,)), sem((YS,)), sem((ZS,)), sem((ZS,)),
+            sem((TRIPLE,)), sem((TRIPLE,)),
             sem((YS,)), sem((YS,)), sem((YS,)), sem((YS,)),
         ],
         compiler_params=pltpu.CompilerParams(

time: 58.3 us -> 58.3 us (level)
  no operation moved by 1% of the time
where the time goes in v6:
time: 58.3 us; the launch traced here: 58.1 us
  Pallas kernels  55.3 us (95%)
  local copies, waits for them, and re-layouts  1.29 us (2%)
  other arithmetic  0.88 us (2%)
  between operations  0.64 us (1%)
    pallas_call x1, Pallas kernels, body(): pl.pallas_call(functools.partial(kernel, full), out_shape=(jax.ShapeDtype...  55.3 us
    unnamed x2, local copies, waits for them, and re-layouts  1.29 us

profile of v6, /device:TPU:1, one launch (start us, length us, event | category | flops | bytes accessed | tf_op | source)
XLA Modules:
  0.0 58.1 jit_solution(11864101360356488553)
XLA Ops:
  0.6 0.9 %pad_maximum_fusion.field_ref = f32[2,16,8,128]{3,2,1,0:T(8,128)S(1)} fusion(f32[1,16,8,128]{3,2,1,0:T(8,128)} %bitcast.2, f32[1,16,8,128]{3,2,1,0:T(8,128)} %bitcast.3), kind=kLoop, calls=%fused_computation | loop fusion | flops 32768 | bytes 262144 | tf_op jit(solution)/shard_map/stack | solution.py:437
  1.5 55.3 %shard_map.95 = (f32[16,8,128]{2,1,0:T(8,128)S(1)}, f32[16,16,128]{2,1,0:T(8,128)S(1)}) custom-call(f32[2,16,8,128]{3,2,1,0:T(8,128)S(1)} %pad_maximum_fusion.field_ref, f32[2,16,16,256]{3,2,1,0:T(8,128)} %h_hbm.1, bf16[256,384]{1,0:T(8,128)(2,1)} %constant.10.clone.first_hbm, f32[16,2,136,128]{3,2,1,0:T(8,128)} %constant.11.clone.turn_hbm, ...), custom_call_target="tpu_custom_call" | custom-call | flops 400000000 | bytes 2000000 | tf_op jit(solution)/shard_map/pallas_call | solution.py:404
  56.8 0.6 %copy.12 = f32[16,8,128]{2,1,0:T(8,128)} copy(f32[16,8,128]{2,1,0:T(8,128)S(1)} %get-tuple-element.4) | data formatting | bytes 131072
  57.5 0.7 %copy.13 = f32[16,16,128]{2,1,0:T(8,128)} copy(f32[16,16,128]{2,1,0:T(8,128)S(1)} %get-tuple-element.5) | data formatting | bytes 262144
